TPU v7x, 256 devices: a whole 4x4x8 slice. The times are simulated.
256 devices in a mesh: outer: 16 (over z, y_lo), dev: 16 (over x, y_hi, core).
Axes of the slice: x: 4, y: 4 (y_hi: 2, y_lo: 2; y = y_hi * 2 + y_lo), z: 8, core: 2. Of those that a mesh axis runs over, the one named last changes fastest.
Arguments:
- partials: bfloat16 [256, 8192, 256], P(('outer', 'dev')), may hold values from -6 to 6
- p_old: bfloat16 [8192, 1024], P('dev'), may hold values from -0.0625 to 0.0625
- p_new: bfloat16 [8192, 1024], P('dev'), may hold values from -0.0625 to 0.0625
- weight: float32 [8192, 256], P('dev'), may hold values from -4 to 4
- m_old: float32 [1024, 256], P('dev'), may hold values from -96 to 96
- v_old: float32 [1024, 256], P('dev'), may hold values from 32 to 1280
Outputs:
- new_weight: float32 [8192, 256], P('dev')
- m_new: float32 [1024, 256], P('dev')
- v_new: float32 [1024, 256], P('dev')
All inputs are finite; a program needn't handle non-finite values.
Results may differ from a plain program's by a relative error of at most 0.0012.
Values may be sent and summed in bfloat16 or wider, within the bound.
No kernel may reach another device: no remote copies, remote signals or barrier semaphores. Data moves between devices by JAX's collectives and lax.ppermute only.
A program may use at most 128 MiB of HBM per device.

v0:
```python
import jax
import jax.numpy as jnp
from jax import lax
from jax.sharding import PartitionSpec as P

beta_mean = 0.9
beta_square = 0.95
bias_mean = 0.9999734386011124
bias_square = 0.9940794707796659
adam_epsilon = 1e-08
step_scale = 0.5


def on_device(partials, p_old, p_new, weight, m_old, v_old):
    local_grad = partials[0].astype(jnp.float32)
    grad_cols = lax.psum_scatter(local_grad, "dev", scatter_dimension=1, tiled=True)
    proj_cols = jnp.dot(
        lax.all_gather(p_new, "dev", axis=0, tiled=True).astype(jnp.float32).T,
        grad_cols,
        precision=lax.Precision.HIGHEST,
    )
    proj_cols = lax.psum(proj_cols, "outer")
    projected = lax.all_to_all(proj_cols, "dev", split_axis=0, concat_axis=1, tiled=True)
    columns = p_new
    margin_rows = lax.psum_scatter(
        jnp.dot(columns.T, p_old, preferred_element_type=jnp.float32),
        "dev",
        scatter_dimension=0,
        tiled=True,
    )
    first_piece = lax.all_gather(m_old, "dev", axis=0, tiled=True)
    second_piece = lax.all_gather(v_old, "dev", axis=0, tiled=True)
    first = jnp.dot(margin_rows, first_piece, precision=lax.Precision.HIGHEST)
    second = jnp.dot(margin_rows * margin_rows, second_piece, precision=lax.Precision.HIGHEST)
    m_new = beta_mean * first + (1.0 - beta_mean) * projected
    v_new = beta_square * second + (1.0 - beta_square) * projected * projected
    direction = (m_new / bias_mean / (jnp.sqrt(v_new / bias_square) + adam_epsilon)).astype(
        jnp.bfloat16
    )
    columns = p_new
    update = jnp.dot(
        columns,
        lax.all_gather(direction, "dev", axis=0, tiled=True),
        preferred_element_type=jnp.float32,
    )
    new_weight = weight - step_scale * update
    return (new_weight, m_new, v_new)


def solution(mesh):
    in_specs = (
        P(("outer", "dev"), None, None),
        P("dev", None),
        P("dev", None),
        P("dev", None),
        P("dev", None),
        P("dev", None),
    )
    out_specs = (P("dev", None), P("dev", None), P("dev", None))
    return jax.shard_map(
        on_device, mesh=mesh, in_specs=in_specs, out_specs=out_specs, check_vma=False
    )
```

profile of v0, /device:TPU:1, one launch (start us, length us, event | category | flops | bytes accessed | tf_op | source)
XLA Modules:
  0.0 627.6 jit_solution(10560370040956481151)
XLA Ops:
  7.2 6.2 bitcast_convert_fusion
  13.4 8.9 %copy.24 = f32[8192,256]{0,1:T(8,128)} copy(f32[8192,256]{1,0:T(8,128)} %bitcast_convert_fusion) | data formatting | bytes 16777216
  22.4 0.7 all-gather.6.cloned.1.call-update
  23.1 112.1 %reduce-scatter.7.cloned.1.call-done = f32[16,8192]{1,0:T(8,128)} async-done(((f32[256,8192]{1,0:T(8,128)}), f32[16,8192]{1,0:T(8,128)}) %reduce-scatter.7.cloned.1.call-update) | async-done | bytes 524304
  135.2 118.6 %all-gather.6.cloned.1.call-done = bf16[8192,1024]{1,0:T(8,128)(2,1)} async-done(((bf16[512,1024]{1,0:T(8,128)(2,1)}), bf16[8192,1024]{1,0:T(8,128)(2,1)}) %all-gather.6.cloned.1.call-update) | async-done | bytes 16777232 | tf_op jit(solution)/shard_map/all_gather | solution.py:18
  253.8 10.2 %fusion.4 = f32[1024,16]{0,1:T(8,128)S(1)} fusion(bf16[8192,1024]{1,0:T(8,128)(2,1)} %all-gather.6.cloned.1.call-done, f32[16,8192]{1,0:T(8,128)} %reduce-scatter.7.cloned.1.call-done), kind=kOutput, calls=%fused_computation.8 | convolution fusion | flops 1610612736 | bytes 17367040 | tf_op jit(solution)/shard_map/dot_general | solution.py:17
  264.1 0.7 copy.18
  264.9 0.5 all-gather.4.cloned.1.call-update
  265.5 3.2 fusion.7
  268.8 0.5 all-gather.8.cloned.1.call-update
  269.4 118.0 %all-reduce.2.cloned.1.call-done = f32[16,64,16]{1,2,0:T(8,128)} async-done(((f32[16,64,16]{1,2,0:T(8,128)}), f32[16,64,16]{1,2,0:T(8,128)}) %all-reduce.2.cloned.1.call-update) | async-done | bytes 65552 | tf_op jit(solution)/shard_map/psum | solution.py:22
  387.4 1.7 reshape.14
  389.0 17.0 %all-to-all-start = ((f32[16,1,1024]{2,1,0:T(1,128)}), f32[16,1,1024]{2,1,0:T(1,128)S(1)}, u32[]{:S(2)}, u32[]{:S(2)}) async-start(f32[16,1,1024]{2,1,0:T(1,128)} %reshape.14), calls=%async_computation.1 | async-start | bytes 131072 | tf_op jit(solution)/shard_map/all_to_all | solution.py:23
  406.2 7.2 %all-to-all-done = f32[16,1,1024]{2,1,0:T(1,128)S(1)} async-done(((f32[16,1,1024]{2,1,0:T(1,128)}), f32[16,1,1024]{2,1,0:T(1,128)S(1)}, u32[]{:S(2)}, u32[]{:S(2)}) %all-to-all-start) | async-done | bytes 65568 | tf_op jit(solution)/shard_map/all_to_all | solution.py:23
  413.4 0.5 broadcast.4
  413.9 0.8 reduce
  414.9 35.6 %all-gather.4.cloned.1.call-done = f32[1024,256]{1,0:T(8,128)} async-done(((f32[64,256]{1,0:T(8,128)}), f32[1024,256]{1,0:T(8,128)}) %all-gather.4.cloned.1.call-update) | async-done | bytes 1048592 | tf_op jit(solution)/shard_map/all_gather | solution.py:31
  450.5 89.9 %reduce-scatter.5.cloned.1.call-done = f32[64,1024]{1,0:T(8,128)} async-done(((f32[1024,1024]{1,0:T(8,128)}), f32[64,1024]{1,0:T(8,128)}) %reduce-scatter.5.cloned.1.call-update) | async-done | bytes 262160 | tf_op jit(solution)/shard_map/reduce_scatter | solution.py:25
  540.3 1.9 fusion.3
  542.3 51.5 %all-gather.8.cloned.1.call-done = f32[1024,256]{1,0:T(8,128)} async-done(((f32[64,256]{1,0:T(8,128)}), f32[1024,256]{1,0:T(8,128)}) %all-gather.8.cloned.1.call-update) | async-done | bytes 1048592 | tf_op jit(solution)/shard_map/all_gather | solution.py:32
  593.8 2.6 divide_convert_fusion
  596.4 22.9 %all_gather.15 = bf16[1024,256]{1,0:T(8,128)(2,1)S(1)} all-gather(bf16[64,256]{1,0:T(8,128)(2,1)S(1)} %get-tuple-element.12), channel_id=1, replica_groups=mesh['outer'=16,'dev'=16] {'dev'}, dimensions={0}, use_global_device_ids=true | all-gather | bytes 557056 | tf_op jit(solution)/shard_map/all_gather | solution.py:43
  619.3 0.5 fusion.1
  619.8 1.0 copy.23
  (21 shorter events, 0.8 us)
Async XLA Ops:
  7.2 258.3 %copy-start = (bf16[512,1024]{1,0:T(8,128)(2,1)S(1)}, bf16[512,1024]{1,0:T(8,128)(2,1)}, u32[]{:S(2)}) copy-start(bf16[512,1024]{1,0:T(8,128)(2,1)} %param.7) | copy-start | bytes 3145732
  7.2 128.1 %reduce-scatter.7.cloned.1.call-start = ((), (), s32[]{:S(2)}) async-start(), calls=%async_computation.8 | async-start | bytes 8912896
  22.3 231.5 %all-gather.6.cloned.1.call-start = ((), (), s32[]{:S(2)}) async-start(), calls=%async_computation.5 | async-start | bytes 17825792 | tf_op jit(solution)/shard_map/all_gather | solution.py:18
  23.1 242.4 %copy-start.1 = (bf16[512,1024]{1,0:T(8,128)(2,1)S(1)}, bf16[512,1024]{1,0:T(8,128)(2,1)}, u32[]{:S(2)}) copy-start(bf16[512,1024]{1,0:T(8,128)(2,1)} %param.8) | copy-start | bytes 3145732
  23.1 364.3 %all-reduce.2.cloned.1.call-start = ((), (), s32[]{:S(2)}) async-start(), calls=%async_computation.6 | async-start | bytes 262144 | tf_op jit(solution)/shard_map/psum | solution.py:22
  264.1 142.0 %copy-start.2 = (f32[512,256]{1,0:T(8,128)S(1)}, f32[512,256]{1,0:T(8,128)}, u32[]{:S(2)}) copy-start(f32[512,256]{1,0:T(8,128)} %param.9) | copy-start | bytes 1572868
  264.9 185.6 %all-gather.4.cloned.1.call-start = ((), (), s32[]{:S(2)}) async-start(), calls=%async_computation.4 | async-start | bytes 1114112 | tf_op jit(solution)/shard_map/all_gather | solution.py:31
  265.5 274.9 %reduce-scatter.5.cloned.1.call-start = ((), (), s32[]{:S(2)}) async-start(), calls=%async_computation.3 | async-start | bytes 4456448 | tf_op jit(solution)/shard_map/reduce_scatter | solution.py:25
  268.8 325.0 %all-gather.8.cloned.1.call-start = ((), (), s32[]{:S(2)}) async-start(), calls=%async_computation.7 | async-start | bytes 1114112 | tf_op jit(solution)/shard_map/all_gather | solution.py:32
  389.0 24.4 %all-to-all-start = ((f32[16,1,1024]{2,1,0:T(1,128)}), f32[16,1,1024]{2,1,0:T(1,128)S(1)}, u32[]{:S(2)}, u32[]{:S(2)}) async-start(f32[16,1,1024]{2,1,0:T(1,128)} %reshape.14), calls=%async_computation.1 | async-start | bytes 131072 | tf_op jit(solution)/shard_map/all_to_all | solution.py:23
  542.3 78.5 %copy-start.3 = (f32[64,256]{1,0:T(8,128)}, f32[64,256]{1,0:T(8,128)S(1)}, u32[]{:S(2)}) copy-start(f32[64,256]{1,0:T(8,128)S(1)} %fusion.3) | copy-start | bytes 196612
Sparse Core Ops, SparseCore 0:
  22.5 112.7 reduce-scatter.6
  137.9 115.8 all-gather.5
  265.0 122.3 all-reduce.1
  390.3 60.1 all-gather.3
  455.3 85.0 reduce-scatter.4
  542.9 50.8 all-gather.7
where the time goes:
time: 628 us
  waiting for transfers between devices  535 us (85%)
  blocking collectives  22.9 us (4%)
  matrix products  18.5 us (3%)
  starting transfers between devices  17.2 us (3%)
  between operations  14.2 us (2%)
  local copies, waits for them, and re-layouts  13.3 us (2%)
  other arithmetic  6.96 us (1%)
    all_gather x1, waiting for transfers between devices, on_device(): lax.all_gather(p_new, 'dev', axis=0, tiled=True).astype(jnp.float32)  119 us
    psum x1, waiting for transfers between devices, on_device(): proj_cols = lax.psum(proj_cols, 'outer')  118 us
    unnamed x7, waiting for transfers between devices  114 us
    reduce_scatter x1, waiting for transfers between devices, on_device(): lax.psum_scatter(jnp.dot(columns.T, p_old, preferred_element_type=jnp.flo...  89.9 us
    all_gather x1, waiting for transfers between devices, on_device(): second_piece = lax.all_gather(v_old, 'dev', axis=0, tiled=True)  51.5 us
    all_gather x1, waiting for transfers between devices, on_device(): first_piece = lax.all_gather(m_old, 'dev', axis=0, tiled=True)  35.6 us
    all_gather x1, blocking collectives, on_device(): lax.all_gather(direction, 'dev', axis=0, tiled=True)  22.9 us
    all_to_all x1, starting transfers between devices, on_device(): lax.all_to_all(proj_cols, 'dev', split_axis=0, concat_axis=1, tiled=True)  17 us
  transfers between devices with their start and end apart: 7, of which 7 were waited for; matrix products, arithmetic and copies ran while one was open for 1% of the time, Pallas kernels for 0%

commit v1 on v0

--- a/solution.py
+++ b/solution.py
@@ -11,6 +11,11 @@
 step_scale = 0.5
 
 
+def add_all(value, name):
+    shards = lax.all_gather(value, name)
+    return jnp.sum(shards, axis=0)
+
+
 def on_device(partials, p_old, p_new, weight, m_old, v_old):
     local_grad = partials[0].astype(jnp.float32)
     grad_cols = lax.psum_scatter(local_grad, "dev", scatter_dimension=1, tiled=True)
@@ -19,7 +24,7 @@
         grad_cols,
         precision=lax.Precision.HIGHEST,
     )
-    proj_cols = lax.psum(proj_cols, "outer")
+    proj_cols = add_all(proj_cols, "outer")
     projected = lax.all_to_all(proj_cols, "dev", split_axis=0, concat_axis=1, tiled=True)
     columns = p_new
     margin_rows = lax.psum_scatter(

time: 628 us -> 562 us (0.89)
  waiting for transfers between devices: 535 us -> 467 us
    psum x1 -> x0, waiting for transfers between devices: 118 us -> none  [on_device(): proj_cols = lax.psum(proj_cols, 'outer')]
    all_gather x0 -> x1, waiting for transfers between devices: none -> 51.5 us  [add_all(): shards = lax.all_gather(value, name)]
    unnamed x13 -> x14, local copies, waits for them, and re-layouts: 11.9 us -> 12.8 us
  transfers between devices with their start and end apart: 7 -> 7, of which waited for: 7 -> 7; matrix products, arithmetic and copies ran while one was open for 1% -> 2% of each run, Pallas kernels for 0% -> 0%
where the time goes in v1:
time: 562 us; the launch traced here: 561 us
  waiting for transfers between devices  467 us (83%)
  blocking collectives  22.9 us (4%)
  matrix products  19.1 us (3%)
  starting transfers between devices  17.7 us (3%)
  between operations  14.2 us (3%)
  local copies, waits for them, and re-layouts  13.5 us (2%)
  other arithmetic  7.11 us (1%)
    all_gather x1, waiting for transfers between devices, on_device(): lax.all_gather(p_new, 'dev', axis=0, tiled=True).astype(jnp.float32)  119 us
    unnamed x7, waiting for transfers between devices  114 us
    reduce_scatter x1, waiting for transfers between devices, on_device(): lax.psum_scatter(jnp.dot(columns.T, p_old, preferred_element_type=jnp.flo...  89.4 us
    all_gather x1, waiting for transfers between devices, on_device(): second_piece = lax.all_gather(v_old, 'dev', axis=0, tiled=True)  51.8 us
    all_gather x1, waiting for transfers between devices, add_all(): shards = lax.all_gather(value, name)  51.5 us
    all_gather x1, waiting for transfers between devices, on_device(): first_piece = lax.all_gather(m_old, 'dev', axis=0, tiled=True)  34.7 us
    all_gather x1, blocking collectives, on_device(): lax.all_gather(direction, 'dev', axis=0, tiled=True)  22.9 us
    all_to_all x1, starting transfers between devices, on_device(): lax.all_to_all(proj_cols, 'dev', split_axis=0, concat_axis=1, tiled=True)  17.4 us
  transfers between devices with their start and end apart: 7, of which 7 were waited for; matrix products, arithmetic and copies ran while one was open for 2% of the time, Pallas kernels for 0%

profile of v1, /device:TPU:1, one launch (start us, length us, event | category | flops | bytes accessed | tf_op | source)
XLA Modules:
  0.0 561.5 jit_solution(1038839888395518812)
XLA Ops:
  7.2 6.2 %bitcast_convert_fusion = f32[8192,256]{1,0:T(8,128)} fusion(bf16[1,8192,256]{2,1,0:T(8,128)(2,1)} %param.6), kind=kLoop, calls=%fused_computation | loop fusion | flops 2097152 | bytes 12582912 | tf_op jit(solution)/shard_map/convert_element_type | solution.py:20
  13.4 8.9 %copy.23 = f32[8192,256]{0,1:T(8,128)} copy(f32[8192,256]{1,0:T(8,128)} %bitcast_convert_fusion) | data formatting | bytes 16777216
  22.4 0.7 all-gather.8.cloned.1.call-update
  23.1 112.1 %reduce-scatter.7.cloned.1.call-done = f32[16,8192]{1,0:T(8,128)} async-done(((f32[256,8192]{1,0:T(8,128)}), f32[16,8192]{1,0:T(8,128)}) %reduce-scatter.7.cloned.1.call-update) | async-done | bytes 524304
  135.2 118.6 %all-gather.8.cloned.1.call-done = bf16[8192,1024]{1,0:T(8,128)(2,1)} async-done(((bf16[512,1024]{1,0:T(8,128)(2,1)}), bf16[8192,1024]{1,0:T(8,128)(2,1)}) %all-gather.8.cloned.1.call-update) | async-done | bytes 16777232 | tf_op jit(solution)/shard_map/all_gather | solution.py:23
  253.8 10.8 %fusion.4 = f32[1024,16]{0,1:T(8,128)} fusion(bf16[8192,1024]{1,0:T(8,128)(2,1)} %all-gather.8.cloned.1.call-done, f32[16,8192]{1,0:T(8,128)} %reduce-scatter.7.cloned.1.call-done), kind=kOutput, calls=%fused_computation.9 | convolution fusion | flops 1610612736 | bytes 17367040 | tf_op jit(solution)/shard_map/dot_general | solution.py:22
  264.8 0.5 all-gather.6.cloned.1.call-update
  265.4 3.2 fusion.7
  268.7 0.5 all-gather.10.cloned.1.call-update
  269.2 51.5 %all-gather.12.cloned.1.call-done = f32[16384,16]{0,1:T(8,128)} async-done(((f32[1024,16]{0,1:T(8,128)}), f32[16384,16]{0,1:T(8,128)}) %all-gather.12.cloned.1.call-update) | async-done | bytes 1048592 | tf_op jit(solution)/shard_map/all_gather | solution.py:15
  320.7 1.8 copy.25
  322.8 0.8 reshape.15
  323.6 17.4 %all-to-all-start = ((f32[16,1,1024]{2,1,0:T(1,128)}), f32[16,1,1024]{2,1,0:T(1,128)S(1)}, u32[]{:S(2)}, u32[]{:S(2)}) async-start(f32[16,1,1024]{2,1,0:T(1,128)} %reshape.15), calls=%async_computation.1 | async-start | bytes 131072 | tf_op jit(solution)/shard_map/all_to_all | solution.py:28
  341.2 7.2 %all-to-all-done = f32[16,1,1024]{2,1,0:T(1,128)S(1)} async-done(((f32[16,1,1024]{2,1,0:T(1,128)}), f32[16,1,1024]{2,1,0:T(1,128)S(1)}, u32[]{:S(2)}, u32[]{:S(2)}) %all-to-all-start) | async-done | bytes 65568 | tf_op jit(solution)/shard_map/all_to_all | solution.py:28
  348.4 0.5 broadcast.4
  348.9 0.8 reduce
  349.9 34.7 %all-gather.6.cloned.1.call-done = f32[1024,256]{1,0:T(8,128)} async-done(((f32[64,256]{1,0:T(8,128)}), f32[1024,256]{1,0:T(8,128)}) %all-gather.6.cloned.1.call-update) | async-done | bytes 1048592 | tf_op jit(solution)/shard_map/all_gather | solution.py:36
  384.6 89.4 %reduce-scatter.5.cloned.1.call-done = f32[64,1024]{1,0:T(8,128)} async-done(((f32[1024,1024]{1,0:T(8,128)}), f32[64,1024]{1,0:T(8,128)}) %reduce-scatter.5.cloned.1.call-update) | async-done | bytes 262160 | tf_op jit(solution)/shard_map/reduce_scatter | solution.py:30
  473.9 1.9 fusion.3
  475.9 51.8 %all-gather.10.cloned.1.call-done = f32[1024,256]{1,0:T(8,128)} async-done(((f32[64,256]{1,0:T(8,128)}), f32[1024,256]{1,0:T(8,128)}) %all-gather.10.cloned.1.call-update) | async-done | bytes 1048592 | tf_op jit(solution)/shard_map/all_gather | solution.py:37
  527.6 2.6 divide_convert_fusion
  530.3 22.9 %all_gather.23 = bf16[1024,256]{1,0:T(8,128)(2,1)S(1)} all-gather(bf16[64,256]{1,0:T(8,128)(2,1)S(1)} %get-tuple-element.12), channel_id=1, replica_groups=mesh['outer'=16,'dev'=16] {'dev'}, dimensions={0}, use_global_device_ids=true | all-gather | bytes 557056 | tf_op jit(solution)/shard_map/all_gather | solution.py:48
  553.1 0.5 fusion.1
  553.6 1.0 copy.22
  (23 shorter events, 1.0 us)
Async XLA Ops:
  7.2 258.2 %copy-start = (bf16[512,1024]{1,0:T(8,128)(2,1)S(1)}, bf16[512,1024]{1,0:T(8,128)(2,1)}, u32[]{:S(2)}) copy-start(bf16[512,1024]{1,0:T(8,128)(2,1)} %param.7) | copy-start | bytes 3145732
  7.2 128.1 %reduce-scatter.7.cloned.1.call-start = ((), (), s32[]{:S(2)}) async-start(), calls=%async_computation.8 | async-start | bytes 8912896
  22.3 231.5 %all-gather.8.cloned.1.call-start = ((), (), s32[]{:S(2)}) async-start(), calls=%async_computation.5 | async-start | bytes 17825792 | tf_op jit(solution)/shard_map/all_gather | solution.py:23
  23.1 242.3 %copy-start.1 = (bf16[512,1024]{1,0:T(8,128)(2,1)S(1)}, bf16[512,1024]{1,0:T(8,128)(2,1)}, u32[]{:S(2)}) copy-start(bf16[512,1024]{1,0:T(8,128)(2,1)} %param.8) | copy-start | bytes 3145732
  23.1 297.6 %all-gather.12.cloned.1.call-start = ((), (), s32[]{:S(2)}) async-start(), calls=%async_computation.7 | async-start | bytes 1114112 | tf_op jit(solution)/shard_map/all_gather | solution.py:15
  264.7 76.3 %copy-start.2 = (f32[512,256]{1,0:T(8,128)S(1)}, f32[512,256]{1,0:T(8,128)}, u32[]{:S(2)}) copy-start(f32[512,256]{1,0:T(8,128)} %param.9) | copy-start | bytes 1572868
  264.7 119.9 %all-gather.6.cloned.1.call-start = ((), (), s32[]{:S(2)}) async-start(), calls=%async_computation.4 | async-start | bytes 1114112 | tf_op jit(solution)/shard_map/all_gather | solution.py:36
  265.3 208.6 %reduce-scatter.5.cloned.1.call-start = ((), (), s32[]{:S(2)}) async-start(), calls=%async_computation.3 | async-start | bytes 4456448 | tf_op jit(solution)/shard_map/reduce_scatter | solution.py:30
  268.6 259.0 %all-gather.10.cloned.1.call-start = ((), (), s32[]{:S(2)}) async-start(), calls=%async_computation.6 | async-start | bytes 1114112 | tf_op jit(solution)/shard_map/all_gather | solution.py:37
  323.6 24.8 %all-to-all-start = ((f32[16,1,1024]{2,1,0:T(1,128)}), f32[16,1,1024]{2,1,0:T(1,128)S(1)}, u32[]{:S(2)}, u32[]{:S(2)}) async-start(f32[16,1,1024]{2,1,0:T(1,128)} %reshape.15), calls=%async_computation.1 | async-start | bytes 131072 | tf_op jit(solution)/shard_map/all_to_all | solution.py:28
  475.9 78.8 %copy-start.3 = (f32[64,256]{1,0:T(8,128)}, f32[64,256]{1,0:T(8,128)S(1)}, u32[]{:S(2)}) copy-start(f32[64,256]{1,0:T(8,128)S(1)} %fusion.3) | copy-start | bytes 196612
Sparse Core Ops, SparseCore 0:
  22.5 112.7 reduce-scatter.6
  137.9 115.8 all-gather.7
  264.8 55.8 all-gather.11
  323.2 61.2 all-gather.5
  388.8 85.1 reduce-scatter.4
  476.8 50.7 all-gather.9
